TPU v7x, 32 devices: a whole 2x2x4 slice. The times are simulated.
32 devices in a mesh: dp: 2 (over y), section: 4 (over x, core), tensor: 4 (over z).
Axes of the slice: x: 2, y: 2, z: 4, core: 2. Of those that a mesh axis runs over, the one named last changes fastest.
Arguments:
- sent_cot: bfloat16 [2, 4, 2, 56, 8192], P('dp', 'section', None, 'tensor'), may hold values from -6 to 6
- saved_heads: bfloat16 [2, 4, 2, 56, 1024], P('dp', 'section', None, None, 'tensor'), may hold values from -0.29882812 to 0.29882812
- out_proj: bfloat16 [4, 8192, 1024], P('section', None, 'tensor'), may hold values from -0.0625 to 0.0625
Outputs:
- head_grads: bfloat16 [2, 4, 2, 56, 1024], P('dp', 'section', None, None, 'tensor')
- proj_grad: bfloat16 [4, 8192, 1024], P('section', 'dp', 'tensor')
All inputs are finite; a program needn't handle non-finite values.
Results may differ from a plain program's by a relative error of at most 0.013.
Values may be sent and summed in bfloat16 or wider, within the bound.
A program may use at most 64 MiB of HBM per device.

v0:
```python
import jax
import jax.numpy as jnp
from jax import lax
from jax.sharding import PartitionSpec as P


def from_behind(value, axis, steps):
    count = lax.axis_size(axis)
    pairs = [(source, (source + steps) % count) for source in range(count)]
    return lax.ppermute(value, axis, pairs)


def per_device(sent_cot, saved_heads, out_proj):
    local_cot = sent_cot[0, 0]
    head_rows = saved_heads[0, 0]
    weight = out_proj[0]
    from_above = from_behind(local_cot[0], "section", -1)
    from_below = from_behind(local_cot[1], "section", 1)
    incoming = jnp.stack([from_above, from_below])
    portion = lax.all_gather(incoming, "tensor", axis=1, tiled=True)
    grad_total = jnp.einsum("rkd,rkh->dh", portion, head_rows, preferred_element_type=jnp.float32)
    head_piece = jnp.einsum("rkd,dh->rkh", portion, weight, preferred_element_type=jnp.float32)
    head_total = head_piece
    grad_total, head_total = (grad_total, head_total)
    rounded = grad_total.astype(jnp.bfloat16).astype(jnp.float32)
    proj_share = lax.psum_scatter(
        rounded.astype(jnp.bfloat16), "dp", scatter_dimension=0, tiled=True
    )
    head_out = head_total.astype(jnp.bfloat16)
    return (head_out[None, None], proj_share[None])


def solution(mesh):
    return jax.shard_map(
        per_device,
        mesh=mesh,
        in_specs=(
            P("dp", "section", None, "tensor", None),
            P("dp", "section", None, None, "tensor"),
            P("section", None, "tensor"),
        ),
        out_specs=(P("dp", "section", None, None, "tensor"), P("section", "dp", "tensor")),
        check_vma=False,
    )
```

profile of v0, /device:TPU:0, one launch (start us, length us, event | category | flops | bytes accessed | tf_op | source)
XLA Modules:
  0.0 129.3 jit_solution(666977936013127331)
XLA Ops:
  7.2 0.0 copy-start
  7.2 0.0 all-gather.2.cloned.1.call-start
  7.2 2.1 %fusion.16 = (bf16[1,1,1,14,8192]{4,2,3,1,0:T(2,128)(2,1)S(1)}, bf16[1,1,1,14,8192]{4,2,3,1,0:T(2,128)(2,1)S(1)}) fusion(bf16[1,1,2,14,8192]{4,2,3,1,0:T(2,128)(2,1)} %param.3), kind=kLoop, calls=%fused_computation.12 | loop fusion | bytes 917504 | tf_op jit(solution)/shard_map/slice | solution.py:17
  9.3 0.3 copy.28
  9.6 0.5 collective-permute-start.1
  10.1 0.2 copy.29
  10.4 2.0 %collective-permute-start = (bf16[14,8192]{1,0:T(8,128)(2,1)S(1)}, bf16[14,8192]{1,0:T(8,128)(2,1)S(1)}, u32[]{:S(2)}, u32[]{:S(2)}) collective-permute-start(bf16[14,8192]{1,0:T(8,128)(2,1)S(1)} %bitcast.29), channel_id=1, source_target_pairs={{0,12},{4,0},{8,4},{12,8},{1,13},{5,1},{9,5},{13,9},{2,14},{6,2},{... | collective-permute-start | bytes 688136 | tf_op jit(solution)/shard_map/ppermute | solution.py:10
  12.4 3.7 %collective-permute-done.1 = bf16[14,8192]{1,0:T(8,128)(2,1)S(1)} collective-permute-done((bf16[14,8192]{1,0:T(8,128)(2,1)S(1)}, bf16[14,8192]{1,0:T(8,128)(2,1)S(1)}, u32[]{:S(2)}, u32[]{:S(2)}) %collective-permute-start.1) | collective-permute-done | bytes 229408 | tf_op jit(solution)/shard_map/ppermute | solution.py:10
  16.1 2.6 %collective-permute-done = bf16[14,8192]{1,0:T(8,128)(2,1)S(1)} collective-permute-done((bf16[14,8192]{1,0:T(8,128)(2,1)S(1)}, bf16[14,8192]{1,0:T(8,128)(2,1)S(1)}, u32[]{:S(2)}, u32[]{:S(2)}) %collective-permute-start) | collective-permute-done | bytes 229408 | tf_op jit(solution)/shard_map/ppermute | solution.py:10
  18.7 0.1 pad_maximum_fusion
  18.8 1.2 copy.13
  20.0 0.0 all-gather.2.cloned.1.call-update
  20.1 0.0 reduce-scatter.2.cloned.1.call-start
  20.1 43.2 %all-gather.2.cloned.1.call-done = bf16[2,56,8192]{2,0,1:T(2,128)(2,1)} async-done(((bf16[2,14,8192]{2,0,1:T(2,128)(2,1)}), bf16[2,56,8192]{2,0,1:T(2,128)(2,1)}) %all-gather.2.cloned.1.call-update) | async-done | bytes 1835024 | tf_op jit(solution)/shard_map/all_gather | solution.py:20
  63.3 0.0 copy-done
  63.3 5.8 %fusion = bf16[8192,256]{1,0:T(8,128)(2,1)} fusion(bf16[2,56,8192]{2,0,1:T(2,128)(2,1)} %all-gather.2.cloned.1.call-done, bf16[1,1,2,56,256]{4,3,2,1,0:T(8,128)(2,1)S(1)} %copy-done), kind=kOutput, calls=%fused_computation.1 | convolution fusion | flops 471859200 | bytes 6086656 | tf_op jit(solution)/shard_map/rkd,rkh->dh/dot_general | solution.py:21
  69.1 0.0 copy-start.1
  69.1 0.0 reduce-scatter.2.cloned.1.call-update
  69.1 1.5 %copy-done.1 = bf16[2,56,8192]{2,0,1:T(2,128)(2,1)S(1)} copy-done((bf16[2,56,8192]{2,0,1:T(2,128)(2,1)S(1)}, bf16[2,56,8192]{2,0,1:T(2,128)(2,1)}, u32[]{:S(2)}) %copy-start.1) | copy-done | bytes 1835032
  70.6 5.3 %fusion.10 = bf16[1,1,2,56,256]{4,3,2,1,0:T(8,128)(2,1)} fusion(bf16[1,8192,256]{2,1,0:T(8,128)(2,1)} %param.5, bf16[2,56,8192]{2,0,1:T(2,128)(2,1)S(1)} %copy-done.1), kind=kOutput, calls=%fused_computation.7 | convolution fusion | flops 469790720 | bytes 6086656 | tf_op jit(solution)/shard_map/rkd,dh->rkh/dot_general | solution.py:22
  75.8 46.6 %reduce-scatter.2.cloned.1.call-done = bf16[4096,256]{1,0:T(8,128)(2,1)} async-done(((bf16[8192,256]{1,0:T(8,128)(2,1)}), bf16[4096,256]{1,0:T(8,128)(2,1)}) %reduce-scatter.2.cloned.1.call-update) | async-done | bytes 2097168 | tf_op jit(solution)/shard_map/reduce_scatter | solution.py:26
Async XLA Ops:
  7.2 56.2 %copy-start = (bf16[1,1,2,56,256]{4,3,2,1,0:T(8,128)(2,1)S(1)}, bf16[1,1,2,56,256]{4,3,2,1,0:T(8,128)(2,1)}, u32[]{:S(2)}) copy-start(bf16[1,1,2,56,256]{4,3,2,1,0:T(8,128)(2,1)} %param.4) | copy-start | bytes 172036
  7.2 56.1 %all-gather.2.cloned.1.call-start = ((), (), s32[]{:S(2)}) async-start(), calls=%async_computation.1 | async-start | bytes 2293760 | tf_op jit(solution)/shard_map/all_gather | solution.py:20
  9.6 6.5 %collective-permute-start.1 = (bf16[14,8192]{1,0:T(8,128)(2,1)S(1)}, bf16[14,8192]{1,0:T(8,128)(2,1)S(1)}, u32[]{:S(2)}, u32[]{:S(2)}) collective-permute-start(bf16[14,8192]{1,0:T(8,128)(2,1)S(1)} %bitcast.27), channel_id=1, source_target_pairs={{0,4},{4,8},{8,12},{12,0},{1,5},{5,9},{9,13},{13,1},{2,6},{6,10},{... | collective-permute-start | bytes 688136 | tf_op jit(solution)/shard_map/ppermute | solution.py:10
  10.4 8.4 %collective-permute-start = (bf16[14,8192]{1,0:T(8,128)(2,1)S(1)}, bf16[14,8192]{1,0:T(8,128)(2,1)S(1)}, u32[]{:S(2)}, u32[]{:S(2)}) collective-permute-start(bf16[14,8192]{1,0:T(8,128)(2,1)S(1)} %bitcast.29), channel_id=1, source_target_pairs={{0,12},{4,0},{8,4},{12,8},{1,13},{5,1},{9,5},{13,9},{2,14},{6,2},{... | collective-permute-start | bytes 688136 | tf_op jit(solution)/shard_map/ppermute | solution.py:10
  20.1 102.4 %reduce-scatter.2.cloned.1.call-start = ((), (), s32[]{:S(2)}) async-start(), calls=%async_computation.2 | async-start | bytes 6291456 | tf_op jit(solution)/shard_map/reduce_scatter | solution.py:26
  69.1 1.5 %copy-start.1 = (bf16[2,56,8192]{2,0,1:T(2,128)(2,1)S(1)}, bf16[2,56,8192]{2,0,1:T(2,128)(2,1)}, u32[]{:S(2)}) copy-start(bf16[2,56,8192]{2,0,1:T(2,128)(2,1)} %all-gather.2.cloned.1.call-done) | copy-start | bytes 5505028
Sparse Core Ops, SparseCore 0:
  20.2 43.0 all-gather.1
  69.2 53.1 reduce-scatter.1
where the time goes:
time: 130 us; the launch traced here: 129 us
  waiting for transfers between devices  96.2 us (74%)
  between operations  14.1 us (11%)
  matrix products  11 us (8%)
  local copies, waits for them, and re-layouts  5.34 us (4%)
  starting transfers between devices  2.58 us (2%)
    reduce_scatter x1, waiting for transfers between devices, per_device(): lax.psum_scatter(rounded.astype(jnp.bfloat16), 'dp', scatter_dimension=0,...  46.6 us
    all_gather x1, waiting for transfers between devices, per_device(): portion = lax.all_gather(incoming, 'tensor', axis=1, tiled=True)  43.2 us
    ppermute x2, waiting for transfers between devices, from_behind(): return lax.ppermute(value, axis, pairs)  6.36 us
    dot_general x1, matrix products, per_device(): jnp.einsum('rkd,rkh->dh', portion, head_rows, preferred_element_type=jnp....  5.75 us
    dot_general x1, matrix products, per_device(): jnp.einsum('rkd,dh->rkh', portion, weight, preferred_element_type=jnp.flo...  5.27 us
  transfers between devices with their start and end apart: 4, of which 4 were waited for; matrix products, arithmetic and copies ran while one was open for 4% of the time, Pallas kernels for 0%

commit v1 on v0

--- a/solution.py
+++ b/solution.py
@@ -2,6 +2,18 @@
 import jax.numpy as jnp
 from jax import lax
 from jax.sharding import PartitionSpec as P
+
+
+def doubled_up(array, axis, dim):
+    ways, here = (lax.axis_size(axis), lax.axis_index(axis))
+    grown, reach = (array, 1)
+    while reach < ways:
+        theirs = lax.ppermute(grown, axis, [(d, d ^ reach) for d in range(ways)])
+        mine_first = jnp.concatenate([grown, theirs], axis=dim)
+        theirs_first = jnp.concatenate([theirs, grown], axis=dim)
+        grown = jnp.where(here & reach == 0, mine_first, theirs_first)
+        reach = 2 * reach
+    return grown
 
 
 def from_behind(value, axis, steps):
@@ -17,7 +29,7 @@
     from_above = from_behind(local_cot[0], "section", -1)
     from_below = from_behind(local_cot[1], "section", 1)
     incoming = jnp.stack([from_above, from_below])
-    portion = lax.all_gather(incoming, "tensor", axis=1, tiled=True)
+    portion = doubled_up(incoming, "tensor", 1)
     grad_total = jnp.einsum("rkd,rkh->dh", portion, head_rows, preferred_element_type=jnp.float32)
     head_piece = jnp.einsum("rkd,dh->rkh", portion, weight, preferred_element_type=jnp.float32)
     head_total = head_piece

time: 130 us -> 144 us (1.11)
  waiting for transfers between devices: 96.2 us -> 111 us
  starting transfers between devices: 2.58 us -> 7 us
  matrix products: 11 us -> 7.2 us
    ppermute x0 -> x2, waiting for transfers between devices: none -> 53 us  [doubled_up(): theirs = lax.ppermute(grown, axis, [(d, d ^ reach) for d in range(ways)])]
    all_gather x1 -> x0, waiting for transfers between devices: 43.2 us -> none  [per_device(): portion = lax.all_gather(incoming, 'tensor', axis=1, tiled=True)]
    reduce_scatter x1, waiting for transfers between devices: 46.6 us -> 51.9 us  [per_device(): lax.psum_scatter(rounded.astype(jnp.bfloat16), 'dp', scatter_dimension=0,...]
    ppermute x0 -> x2, starting transfers between devices: none -> 4.46 us  [doubled_up(): theirs = lax.ppermute(grown, axis, [(d, d ^ reach) for d in range(ways)])]
    dot_general x1, matrix products: 5.75 us -> 3.27 us  [per_device(): jnp.einsum('rkd,rkh->dh', portion, head_rows, preferred_element_type=jnp....]
    unnamed x6 -> x4, local copies, waits for them, and re-layouts: 1.99 us -> 0.51 us
  transfers between devices with their start and end apart: 4 -> 5, of which waited for: 4 -> 5; matrix products, arithmetic and copies ran while one was open for 4% -> 3% of each run, Pallas kernels for 0% -> 0%
where the time goes in v1:
time: 144 us
  waiting for transfers between devices  111 us (77%)
  between operations  14.1 us (10%)
  matrix products  7.2 us (5%)
  starting transfers between devices  7 us (5%)
  local copies, waits for them, and re-layouts  4.08 us (3%)
    ppermute x2, waiting for transfers between devices, doubled_up(): theirs = lax.ppermute(grown, axis, [(d, d ^ reach) for d in range(ways)])  53 us
    reduce_scatter x1, waiting for transfers between devices, per_device(): lax.psum_scatter(rounded.astype(jnp.bfloat16), 'dp', scatter_dimension=0,...  51.9 us
    ppermute x2, waiting for transfers between devices, from_behind(): return lax.ppermute(value, axis, pairs)  6.36 us
    ppermute x2, starting transfers between devices, doubled_up(): theirs = lax.ppermute(grown, axis, [(d, d ^ reach) for d in range(ways)])  4.46 us
    dot_general x1, matrix products, per_device(): jnp.einsum('rkd,dh->rkh', portion, weight, preferred_element_type=jnp.flo...  3.93 us
    dot_general x1, matrix products, per_device(): jnp.einsum('rkd,rkh->dh', portion, head_rows, preferred_element_type=jnp....  3.27 us
  transfers between devices with their start and end apart: 5, of which 5 were waited for; matrix products, arithmetic and copies ran while one was open for 3% of the time, Pallas kernels for 0%

profile of v1, /device:TPU:0, one launch (start us, length us, event | category | flops | bytes accessed | tf_op | source)
XLA Modules:
  0.0 144.2 jit_solution(17994715579120791959)
XLA Ops:
  7.2 0.0 copy-start
  7.2 0.0 reduce-scatter.2.cloned.1.call-start
  7.2 2.1 %fusion.12 = (bf16[1,1,1,14,8192]{4,2,3,1,0:T(2,128)(2,1)S(1)}, bf16[1,1,1,14,8192]{4,2,3,1,0:T(2,128)(2,1)S(1)}) fusion(bf16[1,1,2,14,8192]{4,2,3,1,0:T(2,128)(2,1)} %param.3), kind=kLoop, calls=%fused_computation.14 | loop fusion | bytes 917504 | tf_op jit(solution)/shard_map/slice | solution.py:29
  9.3 0.3 copy.17
  9.6 0.5 collective-permute-start.1
  10.1 0.2 copy.18
  10.4 2.0 %collective-permute-start = (bf16[14,8192]{1,0:T(8,128)(2,1)S(1)}, bf16[14,8192]{1,0:T(8,128)(2,1)S(1)}, u32[]{:S(2)}, u32[]{:S(2)}) collective-permute-start(bf16[14,8192]{1,0:T(8,128)(2,1)S(1)} %bitcast.31), channel_id=1, source_target_pairs={{0,12},{4,0},{8,4},{12,8},{1,13},{5,1},{9,5},{13,9},{2,14},{6,2},{... | collective-permute-start | bytes 688136 | tf_op jit(solution)/shard_map/ppermute | solution.py:22
  12.4 3.7 %collective-permute-done.1 = bf16[14,8192]{1,0:T(8,128)(2,1)S(1)} collective-permute-done((bf16[14,8192]{1,0:T(8,128)(2,1)S(1)}, bf16[14,8192]{1,0:T(8,128)(2,1)S(1)}, u32[]{:S(2)}, u32[]{:S(2)}) %collective-permute-start.1) | collective-permute-done | bytes 229408 | tf_op jit(solution)/shard_map/ppermute | solution.py:22
  16.1 2.6 %collective-permute-done = bf16[14,8192]{1,0:T(8,128)(2,1)S(1)} collective-permute-done((bf16[14,8192]{1,0:T(8,128)(2,1)S(1)}, bf16[14,8192]{1,0:T(8,128)(2,1)S(1)}, u32[]{:S(2)}, u32[]{:S(2)}) %collective-permute-start) | collective-permute-done | bytes 229408 | tf_op jit(solution)/shard_map/ppermute | solution.py:22
  18.7 0.1 pad_maximum_fusion
  18.8 1.6 %collective-permute-start.2 = (bf16[2,14,8192]{2,1,0:T(8,128)(2,1)S(1)}, bf16[2,14,8192]{2,1,0:T(8,128)(2,1)S(1)}, u32[]{:S(2)}, u32[]{:S(2)}) collective-permute-start(bf16[2,14,8192]{2,1,0:T(8,128)(2,1)S(1)} %pad_maximum_fusion), channel_id=1, source_target_pairs={{0,1},{1,0},{2,3},{3,2},{4,5},{5,4},{6,7},{7,6},{8,9},{9,8},{10,11... | collective-permute-start | bytes 1376264 | tf_op jit(solution)/shard_map/ppermute | solution.py:11
  20.4 12.9 %collective-permute-done.2 = bf16[2,14,8192]{2,1,0:T(8,128)(2,1)S(1)} collective-permute-done((bf16[2,14,8192]{2,1,0:T(8,128)(2,1)S(1)}, bf16[2,14,8192]{2,1,0:T(8,128)(2,1)S(1)}, u32[]{:S(2)}, u32[]{:S(2)}) %collective-permute-start.2) | collective-permute-done | bytes 458784 | tf_op jit(solution)/shard_map/ppermute | solution.py:11
  33.3 0.5 maximum_select_fusion.1
  33.8 0.9 copy.10
  34.8 2.8 %collective-permute-start.3 = (bf16[2,28,8192]{2,0,1:T(2,128)(2,1)S(1)}, bf16[2,28,8192]{2,0,1:T(2,128)(2,1)S(1)}, u32[]{:S(2)}, u32[]{:S(2)}) collective-permute-start(bf16[2,28,8192]{2,0,1:T(2,128)(2,1)S(1)} %copy.10), channel_id=1, source_target_pairs={{0,2},{1,3},{2,0},{3,1},{4,6},{5,7},{6,4},{7,5},{8,10},{9,11},{10,... | collective-permute-start | bytes 2752520 | tf_op jit(solution)/shard_map/ppermute | solution.py:11
  37.6 40.1 %collective-permute-done.3 = bf16[2,28,8192]{2,0,1:T(2,128)(2,1)S(1)} collective-permute-done((bf16[2,28,8192]{2,0,1:T(2,128)(2,1)S(1)}, bf16[2,28,8192]{2,0,1:T(2,128)(2,1)S(1)}, u32[]{:S(2)}, u32[]{:S(2)}) %collective-permute-start.3) | collective-permute-done | bytes 917536 | tf_op jit(solution)/shard_map/ppermute | solution.py:11
  77.7 0.5 copy.11
  78.2 0.0 copy-done
  78.2 3.3 %fusion = bf16[8192,256]{1,0:T(8,128)(2,1)} fusion(bf16[2,28,8192]{2,1,0:T(8,128)(2,1)S(1)} %copy.11, bf16[2,28,8192]{2,1,0:T(8,128)(2,1)S(1)} %maximum_select_fusion.1, pred[]{:T(512)S(6)} %eq.6, bf16[1,1,2,56,256]{4,3,2,1,0:T(8,128)(2,1)S(1)} %copy-done), kind=kOutput, calls=%fused_computation.1 | convolution fusion | flops 480116736 | bytes 6086657 | tf_op jit(solution)/shard_map/rkd,rkh->dh/dot_general | solution.py:33
  81.5 0.0 reduce-scatter.2.cloned.1.call-update
  81.5 3.9 %fusion.6 = bf16[1,1,2,56,256]{4,3,2,1,0:T(8,128)(2,1)} fusion(bf16[1,8192,256]{2,1,0:T(8,128)(2,1)} %param.5, bf16[2,28,8192]{2,1,0:T(8,128)(2,1)S(1)} %copy.11, bf16[2,28,8192]{2,1,0:T(8,128)(2,1)S(1)} %maximum_select_fusion.1, pred[]{:T(512)S(6)} %eq.6), kind=kOutput, calls=%fused_computation.6 | convolution fusion | flops 478048256 | bytes 6086657 | tf_op jit(solution)/shard_map/rkd,dh->rkh/dot_general | solution.py:34
  85.5 51.9 %reduce-scatter.2.cloned.1.call-done = bf16[4096,256]{1,0:T(8,128)(2,1)} async-done(((bf16[8192,256]{1,0:T(8,128)(2,1)}), bf16[4096,256]{1,0:T(8,128)(2,1)}) %reduce-scatter.2.cloned.1.call-update) | async-done | bytes 2097168 | tf_op jit(solution)/shard_map/reduce_scatter | solution.py:38
Async XLA Ops:
  7.2 71.1 %copy-start = (bf16[1,1,2,56,256]{4,3,2,1,0:T(8,128)(2,1)S(1)}, bf16[1,1,2,56,256]{4,3,2,1,0:T(8,128)(2,1)}, u32[]{:S(2)}) copy-start(bf16[1,1,2,56,256]{4,3,2,1,0:T(8,128)(2,1)} %param.4) | copy-start | bytes 172036
  7.2 130.2 %reduce-scatter.2.cloned.1.call-start = ((), (), s32[]{:S(2)}) async-start(), calls=%async_computation.1 | async-start | bytes 6291456 | tf_op jit(solution)/shard_map/reduce_scatter | solution.py:38
  9.6 6.5 %collective-permute-start.1 = (bf16[14,8192]{1,0:T(8,128)(2,1)S(1)}, bf16[14,8192]{1,0:T(8,128)(2,1)S(1)}, u32[]{:S(2)}, u32[]{:S(2)}) collective-permute-start(bf16[14,8192]{1,0:T(8,128)(2,1)S(1)} %bitcast.30), channel_id=1, source_target_pairs={{0,4},{4,8},{8,12},{12,0},{1,5},{5,9},{9,13},{13,1},{2,6},{6,10},{... | collective-permute-start | bytes 688136 | tf_op jit(solution)/shard_map/ppermute | solution.py:22
  10.4 8.4 %collective-permute-start = (bf16[14,8192]{1,0:T(8,128)(2,1)S(1)}, bf16[14,8192]{1,0:T(8,128)(2,1)S(1)}, u32[]{:S(2)}, u32[]{:S(2)}) collective-permute-start(bf16[14,8192]{1,0:T(8,128)(2,1)S(1)} %bitcast.31), channel_id=1, source_target_pairs={{0,12},{4,0},{8,4},{12,8},{1,13},{5,1},{9,5},{13,9},{2,14},{6,2},{... | collective-permute-start | bytes 688136 | tf_op jit(solution)/shard_map/ppermute | solution.py:22
  18.8 14.5 %collective-permute-start.2 = (bf16[2,14,8192]{2,1,0:T(8,128)(2,1)S(1)}, bf16[2,14,8192]{2,1,0:T(8,128)(2,1)S(1)}, u32[]{:S(2)}, u32[]{:S(2)}) collective-permute-start(bf16[2,14,8192]{2,1,0:T(8,128)(2,1)S(1)} %pad_maximum_fusion), channel_id=1, source_target_pairs={{0,1},{1,0},{2,3},{3,2},{4,5},{5,4},{6,7},{7,6},{8,9},{9,8},{10,11... | collective-permute-start | bytes 1376264 | tf_op jit(solution)/shard_map/ppermute | solution.py:11
  34.8 43.0 %collective-permute-start.3 = (bf16[2,28,8192]{2,0,1:T(2,128)(2,1)S(1)}, bf16[2,28,8192]{2,0,1:T(2,128)(2,1)S(1)}, u32[]{:S(2)}, u32[]{:S(2)}) collective-permute-start(bf16[2,28,8192]{2,0,1:T(2,128)(2,1)S(1)} %copy.10), channel_id=1, source_target_pairs={{0,2},{1,3},{2,0},{3,1},{4,6},{5,7},{6,4},{7,5},{8,10},{9,11},{10,... | collective-permute-start | bytes 2752520 | tf_op jit(solution)/shard_map/ppermute | solution.py:11
Sparse Core Ops, SparseCore 0:
  81.7 55.6 reduce-scatter.1
